TPU v7x, 32 devices: a whole 2x2x4 slice. The times are simulated.
32 devices in a mesh: dp: 8 (over z, y), tensor: 4 (over x, core).
Axes of the slice: x: 2, y: 2, z: 4, core: 2. Of those that a mesh axis runs over, the one named last changes fastest.
Arguments:
- tokens: bfloat16 [16384, 1536], P(('dp', 'tensor')), may hold values from -6 to 6
- w_query: bfloat16 [1536, 1536], P('dp', 'tensor'), may hold values from -0.15625 to 0.15625
- w_keyval: bfloat16 [1536, 256], P('dp'), may hold values from -0.15625 to 0.15625
- w_out: bfloat16 [1536, 1536], P('tensor', 'dp'), may hold values from -0.625 to 0.625
- w_gate: bfloat16 [1536, 4608], P('dp', 'tensor'), may hold values from -0.15625 to 0.15625
- w_up: bfloat16 [1536, 4608], P('dp', 'tensor'), may hold values from -0.15625 to 0.15625
- w_down: bfloat16 [4608, 1536], P('tensor', 'dp'), may hold values from -0.09375 to 0.09375
- norm_gains: bfloat16 [2, 1536], P(None, 'dp'), may hold values from 0.25 to 1.75
- segment_ids: int32 [16384], P('dp'), may hold values from 0 to 2048, as said below
- grad_output: float32 [16384, 1536], P(('dp', 'tensor')), may hold values from -6 to 6
Outputs:
- output: bfloat16 [16384, 1536], P(('dp', 'tensor'))
- grad_tokens: float32 [16384, 1536], P(('dp', 'tensor'))
- grad_w_query: float32 [1536, 1536], P('dp', 'tensor')
- grad_w_keyval: float32 [1536, 256], P('dp')
- grad_w_out: float32 [1536, 1536], P('tensor', 'dp')
- grad_w_gate: float32 [1536, 4608], P('dp', 'tensor')
- grad_w_up: float32 [1536, 4608], P('dp', 'tensor')
- grad_w_down: float32 [4608, 1536], P('tensor', 'dp')
- grad_norm_gains: float32 [2, 1536], P(None, 'dp')
Inputs may be any that keep to these rules, and one draw needn't show every extreme that they name: `segment_ids`: within each sequence of 2048 tokens the ids never fall except to 0; 0 marks padding, which only ends a sequence; a change of id starts a new document; the last document of every sequence has id 2048.
All inputs are finite; a program needn't handle non-finite values.
Results may differ from a plain program's by a relative error of at most 0.014.
Values may be sent and summed in bfloat16 or wider, within the bound.
A program may use at most 192 MiB of HBM per device.

v0:
```python
import functools

import jax
import jax.numpy as jnp
from jax import lax
from jax.experimental import pallas as pl
from jax.experimental.pallas import tpu as pltpu
from jax.sharding import PartitionSpec as P

WINDOW = 1024
EPS = 1e-6
MASKED = -1e30
HEAD = 128
BLK = 256
LOG2E = 1.4426950408889634
F32 = jnp.float32
BF16 = jnp.bfloat16
MIB = 1 << 20
EARLY = 2

NT = (((1,), (1,)), ((), ()))
TN = (((0,), (0,)), ((), ()))


def dot(left, right):
    return jnp.dot(left, right, preferred_element_type=F32)


def dot_nt(left, right):
    return lax.dot_general(left, right, NT, preferred_element_type=F32)


def dot_tn(left, right):
    return lax.dot_general(left, right, TN, preferred_element_type=F32)


def stacked(block, heads):
    return jnp.concatenate([block[:, h * HEAD : (h + 1) * HEAD] for h in range(heads)], axis=0)


def partner(t, j):
    rem, div = lax.rem, lax.div
    two = jnp.int32(2)
    j = jnp.int32(j)
    return rem(div(t, two) + div(j, two), two) * 2 + rem(rem(t, two) + rem(j, two), two)


def block_rows(i):
    return pl.ds(pl.multiple_of(i * BLK, BLK), BLK)


def key_row(t, kb):
    per = 512 // BLK
    return pl.multiple_of((partner(t, lax.div(kb, per)) * per + lax.rem(kb, per)) * BLK, BLK)


def query_block(t, i):
    per = 512 // BLK
    i = jnp.int32(i)
    return partner(t, lax.div(i, per)) * per + lax.rem(i, per)


def tiled3(row, heads):
    return jnp.concatenate([row] * heads, axis=1)


def attend(t, i, q, k, v, pos, valid, mixed, lse):
    cols = q.shape[1]
    heads = cols // HEAD
    wide = heads * BLK
    qb = query_block(t, i)
    mine = pl.ds(pl.multiple_of(i * BLK, BLK), BLK)
    q3 = stacked(q[mine, :], heads)
    at = qb * BLK + lax.broadcasted_iota(jnp.int32, (1, BLK), 1)
    low = at - jnp.minimum(pos[i], WINDOW - 1)
    at3, low3 = tiled3(at, heads), tiled3(low, heads)
    factor = HEAD**-0.5 * LOG2E

    def step(kb, carry):
        peak, total, acc = carry
        row = key_row(t, kb)
        s = dot_nt(k[pl.ds(row, BLK), :], q3) * factor
        u = kb * BLK + lax.broadcasted_iota(jnp.int32, (BLK, wide), 0)
        s = jnp.where((u <= at3) & (u >= low3), s, MASKED)
        new_peak = jnp.maximum(peak, jnp.max(s, axis=0, keepdims=True))
        p = jnp.exp2(s - new_peak)
        shrink = jnp.exp2(peak - new_peak)
        total = total * shrink + jnp.sum(p, axis=0, keepdims=True)
        acc = acc * shrink + dot_tn(v[pl.ds(row, BLK), :], p.astype(BF16))
        return new_peak, total, acc

    peak, total, acc = lax.fori_loop(
        jnp.maximum(qb - WINDOW // BLK, 0),
        qb + 1,
        step,
        (
            jnp.full((1, wide), MASKED, F32),
            jnp.zeros((1, wide), F32),
            jnp.zeros((HEAD, wide), F32),
        ),
    )
    lse[i] = peak + jnp.log2(total)
    acc = acc * (tiled3(valid[i], heads) / total)
    mixed[mine, :] = jnp.concatenate(
        [acc[:, h * BLK : (h + 1) * BLK].T for h in range(heads)], axis=1
    ).astype(BF16)


def ring_device(p, n):
    p = lax.rem(p + n, jnp.int32(n))
    down = lax.div(p, jnp.int32(n // 2))
    return (1 - down) * 2 * p + down * (2 * (n - 1 - p) + 1)


def ring_place(d, n):
    z, y = lax.div(d, jnp.int32(2)), lax.rem(d, jnp.int32(2))
    return z + y * (n - 1 - 2 * z)


def send(src, dst, sems, at, device):
    return pltpu.make_async_remote_copy(
        src_ref=src,
        dst_ref=dst,
        send_sem=sems.at[0, at],
        recv_sem=sems.at[1, at],
        device_id=device,
        device_id_type=pl.DeviceIdType.MESH,
    )


class Ring:
    def __init__(self, shard, full, sems, first_sem, own, n, direction):
        self.shard, self.full, self.sems, self.at, self.own = shard, full, sems, first_sem, own
        self.n, self.dir = n, direction
        self.copies = {}

    def block(self, offset, place):
        rows = self.shard.shape[0]
        at = ring_device(place + offset * self.dir, self.n) * rows
        return self.full.at[pl.ds(pl.multiple_of(at, rows & -rows), rows), :]

    def begin(self, place):
        self.place = place
        if self.n == 8:
            target = self.block(0, place)
        else:
            target = self.full
        self.local = pltpu.make_async_copy(self.shard, target, self.own)
        self.local.start()
        self.start(1)

    def start(self, s):
        if self.n != 8:
            return
        for way in (0, 1):
            if s > self.n // 2 - way:
                continue
            sign = 1 - 2 * way
            block = self.block(-sign * (s - 1), self.place)
            device = ring_device(self.place + sign * self.dir, self.n)
            src = self.shard if s == 1 else block
            at = self.at + 2 * (s - 1) + way
            copy = send(src, block, self.sems, at, {"dp": device})
            copy.start()
            self.copies[s, way] = copy

    def arrived(self, s):
        for way in (0, 1):
            if (s, way) in self.copies:
                self.copies[s, way].wait_recv()

    def next(self, s):
        self.arrived(s)
        self.start(s + 1)

    def end(self):
        for copy in self.copies.values():
            copy.wait_send()
        self.local.wait()


class RingSum:
    def __init__(self, full, recv, sems, first_sem, n, direction, place, first_hop=1):
        self.full, self.recv, self.sems, self.at = full, recv, sems, first_sem
        self.n, self.dir, self.place, self.first_hop = n, direction, place, first_hop
        self.rows = full.shape[0] // n
        self.copies = {}

    def block(self, offset):
        at = ring_device(self.place + offset * self.dir, self.n) * self.rows
        return pl.ds(pl.multiple_of(at, self.rows & -self.rows), self.rows)

    def last(self, way):
        return self.n // 2 - way

    def slot(self, s, way):
        return way * (self.recv.shape[0] // 2) + s - self.first_hop

    def start(self, s, ways=(0, 1), source=None):
        for way in ways:
            if self.n == 8 and s <= self.last(way):
                sign = 1 - 2 * way
                device = ring_device(self.place + sign * self.dir, self.n)
                rows = self.block(sign * (self.last(way) + 1 - s))
                src = (self.full if source is None else source).at[rows, :]
                slot = self.slot(s, way)
                copy = send(src, self.recv.at[slot], self.sems, self.at + slot, {"dp": device})
                copy.start()
                self.copies[s, way] = copy

    def arrived(self, s, way):
        self.copies[s, way].wait_recv()
        return self.recv[self.slot(s, way)]

    def add(self, s, start=False):
        for way in (0, 1):
            if self.n == 8 and s < self.last(way):
                far = self.last(way)
                mine = self.block((1 - 2 * way) * (far - s))
                self.full[mine, :] = self.full[mine, :] + self.arrived(s, way)
                if start:
                    self.start(s + 1, (way,))

    def next(self, s):
        self.add(s, True)

    def close(self, way):
        if self.n == 8:
            mine = self.block(0)
            self.full[mine, :] = self.full[mine, :] + self.arrived(self.last(way), way)

    def result(self, ways=(0, 1)):
        acc = self.full[self.block(0), :].astype(F32)
        for way in ways:
            acc = acc + self.arrived(self.last(way), way).astype(F32)
        return acc

    def save(self, offsets, target, local):
        if self.n != 8:
            return []
        blocks = [self.block(offset) for offset in offsets]
        return [local(self.full.at[rows, :], target.at[rows, :]) for rows in blocks]

    def end(self):
        for copy in self.copies.values():
            copy.wait_send()


def front_kernel(
    n_dp,
    tokens,
    grad_output,
    shard_a,
    shard_d,
    shard_g,
    pos,
    valid,
    inverse,
    cos_out,
    sin_out,
    w_a_out,
    w_d_out,
    w_g,
    gains,
    normed_out,
    q_out,
    k_out,
    v_out,
    mixed_out,
    lse,
    residual_out,
    n2_out,
    go_out,
    gh_out,
    cos,
    sin,
    w_a,
    w_d,
    x4,
    normed,
    q,
    k,
    v,
    mixed,
    near_recv,
    far_recv,
    x_recv,
    sum_buf,
    n2_own,
    go_buf,
    gh_buf,
    res,
    ring_sems,
    pair_sems,
    local_sems,
):
    quarter, width = tokens.shape
    q_cols = q.shape[1]
    heads = q_cols // HEAD
    kv_at = q_cols + 2 * HEAD
    gain_at = kv_at + q_cols
    t = lax.axis_index("tensor").astype(jnp.int32)
    place = ring_place(lax.axis_index("dp").astype(jnp.int32), n_dp)
    near_id, far_id = {"tensor": partner(t, 1)}, {"tensor": partner(t, 2)}

    barrier = pltpu.get_barrier_semaphore()
    partners = [near_id, far_id]
    if n_dp == 8:
        partners += [{"dp": ring_device(place + 1, n_dp)}, {"dp": ring_device(place - 1, n_dp)}]
    for device in partners:
        pl.semaphore_signal(barrier, inc=1, device_id=device, device_id_type=pl.DeviceIdType.MESH)
    pl.semaphore_wait(barrier, len(partners))

    def rows_of(ref, j, size=1):
        return ref.at[pl.ds(j * quarter, size * quarter), :]

    used = [0]

    def local(src, dst):
        copy = pltpu.make_async_copy(src, dst, local_sems.at[used[0]])
        used[0] += 1
        copy.start()
        return copy

    ring_a = Ring(shard_a, w_a, ring_sems, 0, local_sems.at[24], n_dp, 1)
    ring_d = Ring(shard_d, w_d, ring_sems, 8, local_sems.at[25], n_dp, 1)
    ring_g = Ring(shard_g, w_g, ring_sems, 16, local_sems.at[26], n_dp, -1)

    ring_a.begin(place)
    x_far = send(tokens, rows_of(x4, 2), pair_sems, 0, far_id)
    x_far.start()
    x_near = send(tokens, rows_of(x4, 1), pair_sems, 1, near_id)
    x_near.start()
    x_own = local(tokens, rows_of(x4, 0))
    go_in = local(grad_output, res)
    def tables(i, carry):
        places = jnp.broadcast_to(pos[i].astype(F32), (HEAD, BLK)).T
        angles = places * inverse[...]
        sine = jnp.sin(angles)
        lane = lax.broadcasted_iota(jnp.int32, sine.shape, 1)
        cos[block_rows(i), :] = jnp.cos(angles)
        sin[block_rows(i), :] = jnp.where(lane < HEAD // 2, -sine, sine)
        return carry

    count = pos.shape[0]
    for s in (1, 2, 3):
        lax.fori_loop(count * (s - 1) // 3, count * s // 3, tables, 0)
        ring_a.next(s)
    ring_d.begin(place)
    ring_g.begin(place)
    ring_a.arrived(4)
    ring_a.local.wait()

    gain_rows = w_a[:, gain_at : gain_at + HEAD].astype(F32).T
    gains[...] = gain_rows[:8]

    def project(i, carry):
        mine = pl.ds(pl.multiple_of(i * BLK, BLK), BLK)
        rows = x4[mine, :].astype(F32)
        scale = lax.rsqrt(jnp.mean(rows * rows, axis=-1, keepdims=True) + EPS)
        n = (rows * scale * gains[0:1, :]).astype(BF16)
        normed[mine, :] = n
        y = dot(n, w_a[:, :kv_at])
        c, s = cos[mine, :], sin[mine, :]

        def turned(a):
            return (a * c + pltpu.roll(a, HEAD // 2, 1) * s).astype(BF16)

        q[mine, :] = jnp.concatenate(
            [turned(y[:, h * HEAD : (h + 1) * HEAD]) for h in range(heads)], axis=1
        )
        k[mine, :] = turned(y[:, q_cols : q_cols + HEAD])
        v[mine, :] = y[:, q_cols + HEAD : kv_at].astype(BF16)
        return carry

    per = quarter // BLK
    x_own.wait()
    x_near.wait_recv()
    lax.fori_loop(0, 2 * per, project, 0)
    x_far.wait_recv()
    x_last = send(rows_of(x4, 2), rows_of(x4, 3), pair_sems, 2, near_id)
    x_last.start()
    go_in.wait()
    go_buf[...] = res[...].astype(BF16)
    go_far = send(go_buf, rows_of(go_out, 2), pair_sems, 3, far_id)
    go_far.start()
    go_near = send(go_buf, rows_of(go_out, 1), pair_sems, 4, near_id)
    go_near.start()
    go_own = local(go_buf, rows_of(go_out, 0))
    x_last.wait_recv()
    lax.fori_loop(2 * per, 4 * per, project, 0)
    copies = [
        local(cos, cos_out),
        local(sin, sin_out),
        local(normed, normed_out),
        local(q, q_out),
        local(k, k_out),
        local(v, v_out),
        local(w_a, w_a_out),
    ]

    def attention(i, carry):
        attend(t, i, q, k, v, pos, valid, mixed, lse)
        return carry

    part = x4

    def out_product(i, carry):
        mine = pl.ds(pl.multiple_of(i * BLK, BLK), BLK)
        part[mine, :] = dot_nt(mixed[mine, :], w_a[:, kv_at:gain_at]).astype(BF16)
        return carry

    x_last.wait_send()
    lax.fori_loop(2 * per, 4 * per, attention, 0)
    ring_d.next(1)
    lax.fori_loop(2 * per, 4 * per, out_product, 0)
    part_far = send(rows_of(part, 3), far_recv, pair_sems, 5, near_id)
    part_far.start()
    lax.fori_loop(0, 1, attention, 0)
    part_far.wait_recv()
    sum_buf[...] = (part[pl.ds(2 * quarter, quarter), :].astype(F32) + far_recv[...].astype(F32)).astype(BF16)
    sum_far = send(sum_buf, x_recv, pair_sems, 6, far_id)
    sum_far.start()
    ring_g.next(1)
    lax.fori_loop(1, 2 * per, attention, 0)
    lax.fori_loop(0, 2 * per, out_product, 0)
    part_near = send(rows_of(part, 1), near_recv, pair_sems, 7, near_id)
    part_near.start()
    copies.append(local(mixed, mixed_out))
    ring_d.next(2)
    ring_d.next(3)
    ring_g.next(2)
    go_far.wait_recv()
    go_last = send(rows_of(go_out, 2), rows_of(go_out, 3), pair_sems, 8, near_id)
    go_last.start()
    part_near.wait_recv()
    sum_far.wait_recv()

    res[...] = (
        tokens[...].astype(F32)
        + part[pl.ds(0, quarter), :].astype(F32)
        + near_recv[...].astype(F32)
        + x_recv[...].astype(F32)
    )
    scale_two = lax.rsqrt(jnp.mean(res[...] * res[...], axis=-1, keepdims=True) + EPS)
    n2_own[...] = (res[...] * scale_two * gains[1:2, :]).astype(BF16)
    n2_far = send(n2_own, rows_of(n2_out, 2), pair_sems, 9, far_id)
    n2_far.start()
    n2_near = send(n2_own, rows_of(n2_out, 1), pair_sems, 10, near_id)
    n2_near.start()
    copies.append(local(n2_own, rows_of(n2_out, 0)))
    copies.append(local(res, residual_out))

    ring_d.arrived(4)
    ring_d.local.wait()
    copies.append(local(w_d, w_d_out))
    go_far.wait_send()
    go_near.wait_send()
    go_own.wait()

    def grad_hidden(i, carry):
        mine = pl.ds(pl.multiple_of(i * BLK, BLK), BLK)
        gh_buf[mine, :] = dot(go_buf[mine, :], w_d[...]).astype(BF16)
        return carry

    for j in range(4):
        if j == 1:
            go_near.wait_recv()
        if j == 3:
            go_last.wait_recv()
        if j > 0:
            load = local(rows_of(go_out, j), go_buf)
            load.wait()
        if j > 0:
            store.wait()
        lax.fori_loop(0, per, grad_hidden, 0)
        store = local(gh_buf, rows_of(gh_out, j))
        if j == 1:
            ring_g.next(3)

    n2_far.wait_recv()
    n2_last = send(rows_of(n2_out, 2), rows_of(n2_out, 3), pair_sems, 11, near_id)
    n2_last.start()
    ring_g.arrived(4)
    store.wait()
    for copy in copies:
        copy.wait()
    for copy in (x_far, x_near, part_far, sum_far, part_near, go_last, n2_far, n2_near, n2_last):
        copy.wait_send()
    n2_near.wait_recv()
    n2_last.wait_recv()
    ring_a.copies and [c.wait_send() for c in ring_a.copies.values()]
    ring_d.copies and [c.wait_send() for c in ring_d.copies.values()]
    ring_g.end()


def front(n_dp, tokens, grad_output, shard_a, shard_d, shard_g, pos, valid, inverse, q_cols):
    quarter, width = tokens.shape
    length = 4 * quarter
    heads = q_cols // HEAD
    units = shard_d.shape[1]
    cols_a = shard_a.shape[1]
    vmem = pl.BlockSpec(memory_space=pltpu.VMEM)
    hbm = pl.BlockSpec(memory_space=pl.ANY)
    blocks = length // BLK

    def out(rows, cols, kind=BF16):
        return jax.ShapeDtypeStruct((rows, cols), kind)

    return pl.pallas_call(
        functools.partial(front_kernel, n_dp),
        in_specs=[vmem, hbm, hbm, hbm, hbm, vmem, vmem, vmem],
        out_specs=[hbm, hbm, hbm, hbm, hbm, vmem, hbm, hbm, hbm, hbm, hbm, vmem, hbm, hbm, hbm, hbm],
        out_shape=[
            out(length, HEAD, F32),
            out(length, HEAD, F32),
            out(width, cols_a),
            out(width, units),
            out(width, 2 * units),
            out(8, width, F32),
            out(length, width),
            out(length, q_cols),
            out(length, HEAD),
            out(length, HEAD),
            out(length, q_cols),
            jax.ShapeDtypeStruct((blocks, 1, heads * BLK), F32),
            out(quarter, width, F32),
            out(length, width),
            out(length, width),
            out(length, units),
        ],
        scratch_shapes=[
            pltpu.VMEM((length, HEAD), F32),
            pltpu.VMEM((length, HEAD), F32),
            pltpu.VMEM((width, cols_a), BF16),
            pltpu.VMEM((width, units), BF16),
            pltpu.VMEM((length, width), BF16),
            pltpu.VMEM((length, width), BF16),
            pltpu.VMEM((length, q_cols), BF16),
            pltpu.VMEM((length, HEAD), BF16),
            pltpu.VMEM((length, HEAD), BF16),
            pltpu.VMEM((length, q_cols), BF16),
            pltpu.VMEM((quarter, width), BF16),
            pltpu.VMEM((quarter, width), BF16),
            pltpu.VMEM((quarter, width), BF16),
            pltpu.VMEM((quarter, width), BF16),
            pltpu.VMEM((quarter, width), BF16),
            pltpu.VMEM((quarter, width), BF16),
            pltpu.VMEM((quarter, units), BF16),
            pltpu.VMEM((quarter, width), F32),
            pltpu.SemaphoreType.DMA((2, 24)),
            pltpu.SemaphoreType.DMA((2, 12)),
            pltpu.SemaphoreType.DMA((32,)),
        ],
        compiler_params=pltpu.CompilerParams(
            collective_id=0, has_side_effects=True, vmem_limit_bytes=58 * MIB
        ),
        cost_estimate=pl.CostEstimate(
            flops=12 * length * width * q_cols, bytes_accessed=64 * MIB, transcendentals=0
        ),
        name="front",
    )(tokens, grad_output, shard_a, shard_d, shard_g, pos, valid, inverse)


def attend_back(t, i, q, do, mixed, lse, k, v, pos, valid, cos, sin, dqkv, dk_acc, dv_acc):
    cols = q.shape[1]
    heads = cols // HEAD
    wide = heads * BLK
    qb = query_block(t, i)
    mine = block_rows(i)
    q3 = stacked(q[mine, :], heads)
    do3 = stacked(do[mine, :], heads)
    centre3 = do3.astype(F32) * stacked(mixed[mine, :], heads).astype(F32)
    centre = jnp.sum(centre3.T, axis=0, keepdims=True)
    at = qb * BLK + lax.broadcasted_iota(jnp.int32, (1, BLK), 1)
    low = jnp.where(valid[i] > 0.0, at - jnp.minimum(pos[i], WINDOW - 1), at + 1)
    at3, low3 = tiled3(at, heads), tiled3(low, heads)
    total = lse[i]
    factor = HEAD**-0.5 * LOG2E

    def step(kb, acc):
        row = key_row(t, kb)
        kblk = k[pl.ds(row, BLK), :]
        vblk = v[pl.ds(row, BLK), :]
        s = dot_nt(kblk, q3) * factor - total
        u = kb * BLK + lax.broadcasted_iota(jnp.int32, (BLK, wide), 0)
        p = jnp.exp2(jnp.where((u <= at3) & (u >= low3), s, MASKED))
        gp = dot_nt(vblk, do3)
        ds = (p * (gp - centre)).astype(BF16)
        dv_acc[pl.ds(row, BLK), :] += dot(p.astype(BF16), do3)
        dk_acc[pl.ds(row, BLK), :] += dot(ds, q3)
        return acc + dot_tn(kblk, ds)

    acc = lax.fori_loop(
        jnp.maximum(qb - WINDOW // BLK, 0), qb + 1, step, jnp.zeros((HEAD, wide), F32)
    )
    scale = HEAD**-0.5
    c, sn = cos[mine, :] * scale, sin[mine, :] * scale

    def turned(a):
        return (a * c - pltpu.roll(a, HEAD // 2, 1) * sn).astype(BF16)

    dqkv[mine, :cols] = jnp.concatenate(
        [turned(acc[:, h * BLK : (h + 1) * BLK].T) for h in range(heads)], axis=1
    )


def gated(y, gh, half):
    gate, up = y[:, :half], y[:, half:]
    root = (2.0 / jnp.pi) ** 0.5
    square = gate * gate
    th = jnp.tanh(root * gate * (1.0 + 0.044715 * square))
    one = 0.5 * (1.0 + th)
    act = gate * one
    slope = one + 0.5 * gate * (1.0 - th * th) * (root * (1.0 + 3.0 * 0.044715 * square))
    return (act * up).astype(BF16), (gh * up * slope).astype(BF16), (gh * act).astype(BF16)


def greet(partners):
    barrier = pltpu.get_barrier_semaphore()
    for device in partners:
        pl.semaphore_signal(barrier, inc=1, device_id=device, device_id_type=pl.DeviceIdType.MESH)
    pl.semaphore_wait(barrier, len(partners))


def neighbours(n_dp, t, place):
    near_id, far_id = {"tensor": partner(t, 1)}, {"tensor": partner(t, 2)}
    others = []
    if n_dp == 8:
        others = [{"dp": ring_device(place + 1, n_dp)}, {"dp": ring_device(place - 1, n_dp)}]
    return near_id, far_id, [near_id, far_id] + others


class Local:
    def __init__(self, sems):
        self.sems, self.used = sems, 0

    def __call__(self, src, dst):
        copy = pltpu.make_async_copy(src, dst, self.sems.at[self.used])
        self.used += 1
        copy.start()
        return copy


def middle_kernel(
    n_dp,
    n2_in,
    gh_in,
    go_in,
    w_gu_in,
    w_d_in,
    residual,
    grad_output,
    gains,
    grads_gu_out,
    down_out,
    grad_residual,
    gain_two,
    ga_out,
    ffn_sum_out,
    out_part,
    far_recv,
    x_recv,
    near_recv,
    far_recv2,
    near_recv2,
    w_gu,
    n2,
    go,
    hidden,
    dgu,
    part,
    grads_d,
    grads_gu,
    stage,
    sum_buf,
    ga_own,
    recv_d,
    recv_g,
    rows_a,
    rows_b,
    ring_sems,
    pair_sems,
    local_sems,
):
    length, width = n2.shape
    units = hidden.shape[1]
    quarter = length // 4
    half = length // 2
    t = lax.axis_index("tensor").astype(jnp.int32)
    place = ring_place(lax.axis_index("dp").astype(jnp.int32), n_dp)
    near_id, far_id, partners = neighbours(n_dp, t, place)
    local = Local(local_sems)
    ring_d = RingSum(grads_d, recv_d, ring_sems, 0, n_dp, -1, place)
    ring_g = RingSum(grads_gu, recv_g, ring_sems, 8, n_dp, 1, place)

    far_rows, near_rows = pl.ds(half, half), pl.ds(0, half)
    load_w = local(w_gu_in, w_gu)
    load_far = [local(n2_in.at[far_rows, :], n2.at[far_rows, :]), local(gh_in.at[far_rows, :], hidden.at[far_rows, :])]
    load_near = [local(n2_in.at[near_rows, :], n2.at[near_rows, :]), local(gh_in.at[near_rows, :], hidden.at[near_rows, :])]
    greet(partners)

    def ffn(i, carry):
        mine = block_rows(i)
        y = dot(n2[mine, :], w_gu[...])
        gh = hidden[mine, :].astype(F32)
        hidden[mine, :], dgu[mine, :units], dgu[mine, units:] = gated(y, gh, units)
        return carry

    def back(first):
        def body(i, carry):
            part[block_rows(i), :] = dot_nt(dgu[block_rows(i + first), :], w_gu[...]).astype(BF16)
            return carry

        return body

    def fetch(src, dst):
        local(src, dst).wait()

    upper = pl.ds(quarter, quarter)
    per = half // BLK
    load_w.wait()
    for copy in load_far:
        copy.wait()
    lax.fori_loop(per, 2 * per, ffn, 0)
    lax.fori_loop(0, per, back(per), 0)
    part_far = send(part.at[upper, :], far_recv, pair_sems, 0, near_id)
    part_far.start()
    for copy in load_near:
        copy.wait()
    lax.fori_loop(0, 1, ffn, 0)
    part_far.wait_recv()
    fetch(far_recv, stage)
    sum_buf[...] = (part[:quarter, :].astype(F32) + stage[...].astype(F32)).astype(BF16)
    sum_far = send(sum_buf, x_recv, pair_sems, 1, far_id)
    sum_far.start()
    blocks = width // BLK

    def load_go(i):
        return local(go_in.at[:, pl.ds(i * BLK, BLK)], go.at[i % 2])

    size = rows_a.shape[1]
    steps = quarter // size

    def rows_at(i):
        return pl.ds(i * size, size)

    def load_rows(i):
        return (
            local(residual.at[rows_at(i), :], rows_a.at[i % 2]),
            local(grad_output.at[rows_at(i), :], rows_b.at[i % 2]),
        )

    coming = load_go(0)
    coming_rows = load_rows(0)
    lax.fori_loop(1, per, ffn, 0)
    part_far.wait_send()
    lax.fori_loop(0, per, back(0), 0)
    part_near = send(part.at[upper, :], near_recv, pair_sems, 2, near_id)
    part_near.start()
    load_d = local(w_d_in, w_gu.at[:, :units])

    for i in range(blocks):
        coming.wait()
        if i + 1 < blocks:
            coming = load_go(i + 1)
        grads_d[i * BLK : (i + 1) * BLK, :] = dot_tn(go[i % 2], hidden[...]).astype(BF16)
    ring_d.start(1)

    def gu_grad(i, carry):
        grads_gu[block_rows(i), :] = dot_tn(n2[:, block_rows(i)], dgu[...]).astype(BF16)
        return carry

    part_near.wait_recv()
    fetch(near_recv, stage)
    lax.fori_loop(0, EARLY, gu_grad, 0)
    gain_two[...] = jnp.zeros_like(gain_two)
    sum_far.wait_send()
    sum_far.wait_recv()
    fetch(x_recv, sum_buf)
    stores = []
    for i in range(steps):
        for copy in coming_rows:
            copy.wait()
        if i + 1 < steps:
            if i > 0:
                stores[-1].wait()
            coming_rows = load_rows(i + 1)
        mine = slice(i * size, (i + 1) * size)
        rows = rows_a[i % 2]
        grad_n = part[mine, :].astype(F32) + stage[mine, :].astype(F32) + sum_buf[mine, :].astype(F32)
        scale = lax.rsqrt(jnp.mean(rows * rows, axis=-1, keepdims=True) + EPS)
        weighted = grad_n * gains[1:2, :]
        inner = jnp.mean(rows * weighted, axis=-1, keepdims=True)
        grad = rows_b[i % 2] + scale * weighted - rows * (scale * scale * scale * inner)
        rows_b[i % 2] = grad
        ga_own[mine, :] = grad.astype(BF16)
        gain_two[0:1, :] += jnp.sum(grad_n * rows * scale, axis=0, keepdims=True)
        stores.append(local(rows_b.at[i % 2], grad_residual.at[rows_at(i), :]))

    def quarter_of(ref, j):
        return ref.at[pl.ds(j * quarter, quarter), :]

    ga_far = send(ga_own, quarter_of(ga_out, 2), pair_sems, 3, far_id)
    ga_far.start()
    ga_near = send(ga_own, quarter_of(ga_out, 1), pair_sems, 4, near_id)
    ga_near.start()
    stores_late = [local(ga_own, quarter_of(ga_out, 0))]
    ring_d.next(1)
    lax.fori_loop(EARLY, blocks, gu_grad, 0)
    ring_g.start(1)
    save_gu = local(grads_gu, grads_gu_out)
    ring_d.next(2)
    save_d = local(grads_d, down_out)
    part_near.wait_send()
    load_d.wait()

    def down_product(first):
        def body(i, carry):
            part[block_rows(i), :] = dot_nt(hidden[block_rows(i + first), :], w_gu[:, :units]).astype(BF16)
            return carry

        return body

    lax.fori_loop(0, per, down_product(per), 0)
    part_far2 = send(part.at[upper, :], far_recv2, pair_sems, 5, near_id)
    part_far2.start()
    part_far2.wait_recv()
    fetch(far_recv2, stage)
    sum_buf[...] = (part[:quarter, :].astype(F32) + stage[...].astype(F32)).astype(BF16)
    stores_late.append(local(sum_buf, ffn_sum_out))
    part_far2.wait_send()
    lax.fori_loop(0, per, down_product(0), 0)
    part_near2 = send(part.at[upper, :], near_recv2, pair_sems, 6, near_id)
    part_near2.start()
    part_near2.wait_recv()
    fetch(near_recv2, stage)
    for copy in stores[-2:]:
        copy.wait()
    stores = []
    coming = local(residual.at[rows_at(0), :], rows_a.at[0])
    for i in range(steps):
        coming.wait()
        if i + 1 < steps:
            if i > 0:
                stores[-1].wait()
            coming = local(residual.at[rows_at(i + 1), :], rows_a.at[(i + 1) % 2])
        mine = slice(i * size, (i + 1) * size)
        rows_a[i % 2] = rows_a[i % 2] + part[mine, :].astype(F32) + stage[mine, :].astype(F32)
        stores.append(local(rows_a.at[i % 2], out_part.at[rows_at(i), :]))
    stores_late += stores[-2:]

    ga_far.wait_recv()
    ga_last = send(quarter_of(ga_out, 2), quarter_of(ga_out, 3), pair_sems, 7, near_id)
    ga_last.start()
    save_d.wait()
    ring_d.add(3)
    ring_d.close(1)
    stores_late += ring_d.save((1, 0), down_out, local)
    save_gu.wait()
    ring_g.add(1)
    stores_late += ring_g.save((3, -2), grads_gu_out, local)
    ring_d.end()
    ring_g.end()
    ga_near.wait_recv()
    ga_last.wait_recv()
    for copy in stores_late:
        copy.wait()
    for copy in (ga_far, ga_near, ga_last, part_near2):
        copy.wait_send()


def middle(n_dp, n2, gh, go, w_gu, w_d, residual, grad_output, gains):
    length, width = n2.shape
    units = gh.shape[1]
    quarter = length // 4
    rows = width // 8
    vmem = pl.BlockSpec(memory_space=pltpu.VMEM)
    hbm = pl.BlockSpec(memory_space=pl.ANY)
    shape = jax.ShapeDtypeStruct
    pair = shape((quarter, width), BF16)
    return pl.pallas_call(
        functools.partial(middle_kernel, n_dp),
        in_specs=[hbm] * 7 + [vmem],
        out_specs=[hbm] * 3 + [vmem] + [hbm] * 8,
        out_shape=[
            shape((width, 2 * units), BF16),
            shape((width, units), BF16),
            shape((quarter, width), F32),
            shape((8, width), F32),
            shape((length, width), BF16),
            pair,
            shape((quarter, width), F32),
            pair,
            pair,
            pair,
            pair,
            pair,
        ],
        scratch_shapes=[
            pltpu.VMEM((width, 2 * units), BF16),
            pltpu.VMEM((length, width), BF16),
            pltpu.VMEM((2, length, BLK), BF16),
            pltpu.VMEM((length, units), BF16),
            pltpu.VMEM((length, 2 * units), BF16),
            pltpu.VMEM((length // 2, width), BF16),
            pltpu.VMEM((width, units), BF16),
            pltpu.VMEM((width, 2 * units), BF16),
            pltpu.VMEM((quarter, width), BF16),
            pltpu.VMEM((quarter, width), BF16),
            pltpu.VMEM((quarter, width), BF16),
            pltpu.VMEM((6, rows, units), BF16),
            pltpu.VMEM((2, rows, 2 * units), BF16),
            pltpu.VMEM((2, 128, width), F32),
            pltpu.VMEM((2, 128, width), F32),
            pltpu.SemaphoreType.DMA((2, 16)),
            pltpu.SemaphoreType.DMA((2, 8)),
            pltpu.SemaphoreType.DMA((72,)),
        ],
        compiler_params=pltpu.CompilerParams(
            collective_id=1, has_side_effects=True, vmem_limit_bytes=63 * MIB
        ),
        cost_estimate=pl.CostEstimate(
            flops=14 * length * width * units, bytes_accessed=64 * MIB, transcendentals=0
        ),
        name="middle",
    )(n2, gh, go, w_gu, w_d, residual, grad_output, gains)[:7]


def back_kernel(
    n_dp,
    ga_in,
    grads_gu_in,
    grads_d_in,
    ffn_sum,
    w_a_in,
    q_in,
    k_in,
    v_in,
    mixed_in,
    normed_in,
    lse,
    pos,
    valid,
    cos,
    sin,
    gains,
    gain_two,
    part_own,
    x_recv,
    near_recv,
    x_recv2,
    gate_out,
    up_out,
    down_out,
    grads_a_out,
    keyval_out,
    out_out,
    gain_out,
    far_recv,
    acts,
    w_a,
    q,
    k,
    v,
    mixed,
    do,
    dqkv,
    dk_acc,
    dv_acc,
    grads_a,
    grads_o,
    grads_d,
    grads_gu,
    part,
    stage,
    sum_buf,
    recv_g,
    recv_a,
    recv_o,
    recv_d,
    result_gu,
    result_a,
    result_o,
    result_d,
    gain_acc,
    gain_cols,
    recv_s,
    small,
    small_near,
    small_far,
    ring_sems,
    pair_sems,
    local_sems,
):
    length, width = acts.shape
    quarter = length // 4
    half = length // 2
    q_cols = q.shape[1]
    kv_at = q_cols + 2 * HEAD
    out_at = kv_at + q_cols
    units = grads_gu.shape[1] // 2
    ring = n_dp == 8
    t = lax.axis_index("tensor").astype(jnp.int32)
    place = ring_place(lax.axis_index("dp").astype(jnp.int32), n_dp)
    near_id, far_id, partners = neighbours(n_dp, t, place)
    local = Local(local_sems)
    ring_g = RingSum(grads_gu, recv_g, ring_sems, 0, n_dp, 1, place, 2)
    ring_a = RingSum(grads_a, recv_a, ring_sems, 8, n_dp, -1, place)
    ring_o = RingSum(grads_o, recv_o, ring_sems, 24, n_dp, -1, place)
    ring_d = RingSum(grads_d, recv_d, ring_sems, 32, n_dp, -1, place, 4)
    ring_s = RingSum(gain_cols, recv_s, ring_sems, 16, n_dp, 1, place)

    load_ga, load_w, load_mixed = local(ga_in, acts), local(w_a_in, w_a), local(mixed_in, mixed)
    loads = [local(src, dst) for src, dst in ((q_in, q), (k_in, k), (v_in, v))]
    greet(partners)
    ring_g.start(2, source=grads_gu_in)
    ring_d.start(4, source=grads_d_in)
    sum_far2 = send(ffn_sum, x_recv2, pair_sems, 0, far_id)
    sum_far2.start()
    if ring:
        loads += [local(grads_gu_in, grads_gu), local(grads_d_in, grads_d)]
    load_ga.wait()
    load_w.wait()

    def grad_mixed(i, carry):
        do[block_rows(i), :] = dot(acts[block_rows(i), :], w_a[:, kv_at:out_at]).astype(BF16)
        return carry

    def out_grad(i, carry):
        grads_o[block_rows(i), :] = dot_tn(acts[:, block_rows(i)], mixed[...]).astype(BF16)
        return carry

    blocks = length // BLK
    lax.fori_loop(0, blocks, grad_mixed, 0)
    load_mixed.wait()
    lax.fori_loop(0, width // BLK, out_grad, 0)
    ring_o.start(1)
    load_normed = local(normed_in, acts)
    for copy in loads:
        copy.wait()

    dk_acc[...] = jnp.zeros_like(dk_acc)
    dv_acc[...] = jnp.zeros_like(dv_acc)

    def attention(i, carry):
        attend_back(t, i, q, do, mixed, lse, k, v, pos, valid, cos, sin, dqkv, dk_acc, dv_acc)
        return carry

    lax.fori_loop(0, blocks * 4 // 8, attention, 0)
    ring_o.next(1)
    ring_g.next(2)
    lax.fori_loop(blocks * 4 // 8, blocks * 6 // 8, attention, 0)
    ring_o.next(2)
    if ring:
        result_d[...] = ring_d.result((0,))
        store_d = local(result_d, down_out)
    lax.fori_loop(blocks * 6 // 8, blocks, attention, 0)
    a = dk_acc[...] * HEAD**-0.5
    dqkv[:, q_cols : q_cols + HEAD] = (a * cos[...] - pltpu.roll(a, HEAD // 2, 1) * sin[...]).astype(BF16)
    dqkv[:, q_cols + HEAD : kv_at] = dv_acc[...].astype(BF16)
    load_normed.wait()

    gain_acc[...] = jnp.zeros_like(gain_acc)

    def grad_normed(first):
        def body(i, carry):
            mine = block_rows(i + first)
            y = dot_nt(dqkv[mine, :], w_a[:, :kv_at])
            part[block_rows(i), :] = y.astype(BF16)
            gain_acc[0:1, :] += jnp.sum(y * acts[mine, :].astype(F32), axis=0, keepdims=True)
            return carry

        return body

    def fetch(src, dst):
        local(src, dst).wait()

    upper = pl.ds(quarter, quarter)
    per = half // BLK
    lax.fori_loop(0, per, grad_normed(per), 0)
    part_far = send(part.at[upper, :], far_recv, pair_sems, 1, near_id)
    part_far.start()
    ring_o.next(3)

    def qkv_grad(i, carry):
        grads_a[block_rows(i), :] = dot_tn(acts[:, block_rows(i)], dqkv[...]).astype(BF16)
        return carry

    lax.fori_loop(0, width // BLK, qkv_grad, 0)
    ring_a.start(1)
    part_far.wait_recv()
    fetch(far_recv, stage)
    sum_buf[...] = (part[:quarter, :].astype(F32) + stage[...].astype(F32)).astype(BF16)
    sum_far = send(sum_buf, x_recv, pair_sems, 2, far_id)
    sum_far.start()
    part_far.wait_send()
    lax.fori_loop(0, per, grad_normed(0), 0)
    part_near = send(part.at[upper, :], near_recv, pair_sems, 3, near_id)
    part_near.start()
    stores = [local(part.at[pl.ds(0, quarter), :], part_own)]
    ring_g.next(3)

    both = jnp.concatenate(
        [gain_acc[0:1, :] / gains[0:1, :], gain_two[0:1, :], jnp.zeros((HEAD - 2, width), F32)], axis=0
    )
    gain_cols[...] = both.T
    ring_s.start(1)
    ring_a.next(1)
    ring_s.next(1)
    if ring:
        result_o[...] = ring_o.result()
        stores.append(local(result_o, out_out))
    ring_a.next(2)
    ring_s.next(2)
    if ring:
        result_gu[...] = ring_g.result()
        stores += [local(result_gu.at[:, :units], gate_out), local(result_gu.at[:, units:], up_out)]
    ring_a.next(3)
    ring_s.next(3)

    if ring:
        shard = ring_a.result()
        result_a[:, :q_cols] = shard[:, :q_cols]
        small[:, : 2 * HEAD] = shard[:, q_cols:kv_at].astype(BF16)
        small[:, 2 * HEAD :] = ring_s.result().astype(BF16)
        small_one = send(small, small_near, pair_sems, 4, near_id)
        small_one.start()
        small_one.wait_send()
        small_one.wait_recv()
        small[...] = (small[...].astype(F32) + small_near[...].astype(F32)).astype(BF16)
        small_two = send(small, small_far, pair_sems, 5, far_id)
        small_two.start()
        small_two.wait_send()
        small_two.wait_recv()
        both = small[...].astype(F32) + small_far[...].astype(F32)
        result_a[:, q_cols:kv_at] = both[:, : 2 * HEAD]
        ring_s.end()
        gain_cols[: both.shape[0], :] = both[:, 2 * HEAD :]
        stores.append(local(result_a.at[:, :q_cols], grads_a_out))
        stores.append(local(result_a.at[:, q_cols:], keyval_out))
        stores.append(local(gain_cols.at[pl.ds(0, both.shape[0]), :], gain_out))
    else:
        stores.append(local(grads_a, grads_a_out))
        stores.append(local(result_a.at[:, q_cols:], keyval_out))
        stores.append(local(grads_o, out_out))
        stores.append(local(gain_cols, gain_out))
    if ring:
        stores.append(store_d)
    for copy in stores:
        copy.wait()
    for each in (ring_g, ring_a, ring_o, ring_d):
        each.end()
    for copy in (sum_far2, part_near, sum_far):
        copy.wait_send()
    sum_far2.wait_recv()
    part_near.wait_recv()
    sum_far.wait_recv()


def back(n_dp, ga, grads_gu, grads_d, ffn_sum, w_a, q, k, v, mixed, normed, *rest):
    length, width = ga.shape
    units = grads_gu.shape[1] // 2
    quarter = length // 4
    rows = width // 8
    q_cols = q.shape[1]
    cols = q_cols + 2 * HEAD
    vmem = pl.BlockSpec(memory_space=pltpu.VMEM)
    hbm = pl.BlockSpec(memory_space=pl.ANY)
    shape = jax.ShapeDtypeStruct
    pair = shape((quarter, width), BF16)
    ring = n_dp == 8
    return pl.pallas_call(
        functools.partial(back_kernel, n_dp),
        in_specs=[hbm] * 10 + [vmem] * 7,
        out_specs=[hbm] * 12,
        out_shape=[
            pair,
            pair,
            pair,
            pair,
            shape((rows, units), F32),
            shape((rows, units), F32),
            shape((rows, units), F32),
            shape((rows, q_cols), F32) if ring else shape((width, cols), BF16),
            shape((rows, 2 * HEAD), F32),
            shape((rows, q_cols), F32) if ring else shape((width, q_cols), BF16),
            shape((rows if ring else width, HEAD), F32),
            pair,
        ],
        scratch_shapes=[
            pltpu.VMEM((length, width), BF16),
            pltpu.VMEM(w_a.shape, BF16),
            pltpu.VMEM((length, q_cols), BF16),
            pltpu.VMEM((length, HEAD), BF16),
            pltpu.VMEM((length, HEAD), BF16),
            pltpu.VMEM((length, q_cols), BF16),
            pltpu.VMEM((length, q_cols), BF16),
            pltpu.VMEM((length, q_cols + 2 * HEAD), BF16),
            pltpu.VMEM((length, HEAD), F32),
            pltpu.VMEM((length, HEAD), F32),
            pltpu.VMEM((width, cols), BF16),
            pltpu.VMEM((width, q_cols), BF16),
            pltpu.VMEM((width, units), BF16),
            pltpu.VMEM((width, 2 * units), BF16),
            pltpu.VMEM((length // 2, width), BF16),
            pltpu.VMEM((quarter, width), BF16),
            pltpu.VMEM((quarter, width), BF16),
            pltpu.VMEM((6, rows, 2 * units), BF16),
            pltpu.VMEM((8, rows, cols), BF16),
            pltpu.VMEM((8, rows, q_cols), BF16),
            pltpu.VMEM((2, rows, units), BF16),
            pltpu.VMEM((rows, 2 * units), F32),
            pltpu.VMEM((rows, cols), F32),
            pltpu.VMEM((rows, q_cols), F32),
            pltpu.VMEM((rows, units), F32),
            pltpu.VMEM((8, width), F32),
            pltpu.VMEM((width, HEAD), F32),
            pltpu.VMEM((8, rows, HEAD), F32),
            pltpu.VMEM((rows, 3 * HEAD), BF16),
            pltpu.VMEM((rows, 3 * HEAD), BF16),
            pltpu.VMEM((rows, 3 * HEAD), BF16),
            pltpu.SemaphoreType.DMA((2, 40)),
            pltpu.SemaphoreType.DMA((2, 8)),
            pltpu.SemaphoreType.DMA((72,)),
        ],
        compiler_params=pltpu.CompilerParams(
            collective_id=2, has_side_effects=True, vmem_limit_bytes=60 * MIB
        ),
        cost_estimate=pl.CostEstimate(
            flops=14 * length * width * q_cols, bytes_accessed=64 * MIB, transcendentals=0
        ),
        name="back",
    )(ga, grads_gu, grads_d, ffn_sum, w_a, q, k, v, mixed, normed, *rest)[:11]


def final_kernel(
    own, near, far, ffn_far, out_part, tokens, grad_residual, gains, output, grad_tokens
):
    output[...] = (out_part[...] + ffn_far[...].astype(F32)).astype(BF16)
    rows = tokens[...].astype(F32)
    grad_n = own[...].astype(F32) + near[...].astype(F32) + far[...].astype(F32)
    scale = lax.rsqrt(jnp.mean(rows * rows, axis=-1, keepdims=True) + EPS)
    weighted = grad_n * gains[0:1, :]
    inner = jnp.mean(rows * weighted, axis=-1, keepdims=True)
    grad_tokens[...] = grad_residual[...] + scale * weighted - rows * (scale * scale * scale * inner)


def final(blocks, gains):
    quarter, width = blocks[0].shape
    size = 128
    row = pl.BlockSpec((size, width), lambda i: (i, 0))
    return pl.pallas_call(
        final_kernel,
        grid=(quarter // size,),
        in_specs=[row] * 7 + [pl.BlockSpec((8, width), lambda i: (0, 0))],
        out_specs=[row, row],
        out_shape=[
            jax.ShapeDtypeStruct((quarter, width), BF16),
            jax.ShapeDtypeStruct((quarter, width), F32),
        ],
        compiler_params=pltpu.CompilerParams(vmem_limit_bytes=62 * MIB),
        name="final",
    )(*blocks, gains)


def positions_of(segments):
    places = jnp.arange(segments.shape[0], dtype=jnp.int32)
    previous = jnp.concatenate([jnp.full((1,), -1, jnp.int32), segments[:-1]])
    starts = lax.cummax(jnp.where(segments != previous, places, 0), axis=0)
    return places - starts


def per_device(
    n_dp,
    tokens,
    w_query,
    w_keyval,
    w_out,
    w_gate,
    w_up,
    w_down,
    norm_gains,
    segment_ids,
    grad_output,
):
    t = lax.axis_index("tensor").astype(jnp.int32)
    quarter, width = tokens.shape
    length = 4 * quarter
    q_cols = w_query.shape[1]
    units = w_gate.shape[1]

    gain_cols = jnp.pad(norm_gains.T, ((0, 0), (0, HEAD - 2)))
    shard_a = jnp.concatenate([w_query, w_keyval, w_out.T, gain_cols], axis=1)
    shard_d = w_down.T
    shard_g = jnp.concatenate([w_gate, w_up], axis=1)
    if n_dp != 8:
        shard_a, shard_d, shard_g = (
            lax.all_gather(w, "dp", axis=0, tiled=True) for w in (shard_a, shard_d, shard_g)
        )

    turn = t ^ jnp.arange(4, dtype=jnp.int32)
    positions = positions_of(segment_ids).reshape(4, quarter)[turn].reshape(length)
    valid = (segment_ids != 0).reshape(4, quarter)[turn].reshape(length).astype(F32)
    inverse = 10000.0 ** (-jnp.arange(HEAD // 2, dtype=F32) / (HEAD // 2))
    inverse = jnp.concatenate([inverse, inverse])[None, :]
    pos3 = positions.reshape(length // BLK, 1, BLK)
    valid3 = valid.reshape(length // BLK, 1, BLK)

    (cos, sin, w_a, w_down_t, w_gu, gains, normed, q, k, v, mixed, lse, residual, n2, go_all, gh) = front(
        n_dp, tokens, grad_output, shard_a, shard_d, shard_g, pos3, valid3, inverse, q_cols
    )
    grads_gu, grads_d, grad_residual, gain_two, ga, ffn_sum, out_part = middle(
        n_dp, n2, gh, go_all, w_gu, w_down_t, residual, grad_output, gains
    )
    part_own, part_far, part_near, ffn_far, gate, up, down, grads_a, keyval, out_grads, gain_grads = back(
        n_dp, ga, grads_gu, grads_d, ffn_sum, w_a, q, k, v, mixed, normed,
        lse, pos3, valid3, cos, sin, gains, gain_two
    )
    query = grads_a
    if n_dp != 8:

        def spread(full):
            return lax.psum_scatter(full.astype(F32), "dp", scatter_dimension=0, tiled=True)

        down, gate, up, grads_a, out_grads, gain_grads = (
            spread(w)
            for w in (grads_d, grads_gu[:, :units], grads_gu[:, units:], grads_a, out_grads, gain_grads)
        )
        keyval, gain_grads = lax.psum((grads_a[:, q_cols:], gain_grads), "tensor")
        query = grads_a[:, :q_cols]
    blocks = (part_own, part_near, part_far, ffn_far, out_part, tokens, grad_residual)
    output, grad_tokens = final(blocks, gains)

    return (
        output,
        grad_tokens,
        query,
        keyval,
        out_grads.T,
        gate,
        up,
        down.T,
        gain_grads[:, :2].T,
    )


def solution(mesh):
    return jax.shard_map(
        functools.partial(per_device, mesh.shape["dp"]),
        mesh=mesh,
        in_specs=(
            P(("dp", "tensor"), None),
            P("dp", "tensor"),
            P("dp", None),
            P("tensor", "dp"),
            P("dp", "tensor"),
            P("dp", "tensor"),
            P("tensor", "dp"),
            P(None, "dp"),
            P("dp"),
            P(("dp", "tensor"), None),
        ),
        out_specs=(
            P(("dp", "tensor"), None),
            P(("dp", "tensor"), None),
            P("dp", "tensor"),
            P("dp", None),
            P("tensor", "dp"),
            P("dp", "tensor"),
            P("dp", "tensor"),
            P("tensor", "dp"),
            P(None, "dp"),
        ),
        check_vma=False,
    )
```

profile of v0, /device:TPU:0, one launch (start us, length us, event | category | flops | bytes accessed | tf_op | source)
XLA Modules:
  0.0 428.7 jit_solution(8758279813935580496)
XLA Ops:
  0.7 0.6 maximum_bitcast_fusion.inverse
  1.3 0.7 broadcast_compare_fusion
  2.0 0.6 gather_fusion.1
  2.6 0.6 reshape.80.valid
  3.2 0.8 select_bitcast_fusion
  4.0 0.3 reduce-window.9
  4.3 0.1 slice.21
  4.4 0.1 slice_reduce_fusion
  4.5 0.1 reshape.77
  4.6 0.1 broadcast_bitcast_fusion
  4.7 0.6 gather_fusion
  5.3 0.6 reshape_reshape.3.pos
  5.9 0.8 copy.21
  6.7 1.8 fusion.1.shard_a
  8.6 2.1 pad_maximum_fusion.shard_g
  10.7 165.8 %front.1 = (f32[2048,128]{1,0:T(8,128)}, f32[2048,128]{1,0:T(8,128)}, bf16[1536,1152]{1,0:T(8,128)(2,1)}, bf16[1536,1152]{1,0:T(8,128)(2,1)}, bf16[1536,2304]{1,...) custom-call(bf16[512,1536]{1,0:T(8,128)(2,1)} %tokens.3, ...), custom_call_target="tpu_custom_call" | custom-call | flops 14495514624 | bytes 67108864 | tf_op jit(solution)/shard_map/front/pallas_call | solution.py:510
  176.5 113.3 %middle.1 = (bf16[1536,2304]{1,0:T(8,128)(2,1)}, bf16[1536,1152]{1,0:T(8,128)(2,1)}, f32[512,1536]{1,0:T(8,128)}, f32[8,1536]{1,0:T(8,128)}, bf16[2048,1536]{1,0...) custom-call(bf16[2048,1536]{1,0:T(8,128)(2,1)} %get-tuple-element.45, ...), custom_call_target="tpu_custom_call" | custom-call | flops 50734301184 | bytes 67108864 | tf_op jit(solution)/shard_map/middle/pallas_call | solution.py:882
  289.8 124.2 %back.1 = (bf16[512,1536]{1,0:T(8,128)(2,1)}, bf16[512,1536]{1,0:T(8,128)(2,1)}, bf16[512,1536]{1,0:T(8,128)(2,1)}, bf16[512,1536]{1,0:T(8,128)(2,1)}, f32[192,1...) custom-call(bf16[2048,1536]{1,0:T(8,128)(2,1)} %get-tuple-element.52, ...), custom_call_target="tpu_custom_call" | custom-call | flops 16911433728 | bytes 67108864 | tf_op jit(solution)/shard_map/back/pallas_call | solution.py:1173
  414.1 0.0 copy-start.6
  414.1 0.0 copy-start.4
  414.1 0.0 copy-start.5
  414.1 0.0 copy-start.3
  414.1 8.5 %final.1 = (bf16[512,1536]{1,0:T(8,128)(2,1)}, f32[512,1536]{1,0:T(8,128)}) custom-call(bf16[512,1536]{1,0:T(8,128)(2,1)} %get-tuple-element.66.own, bf16[512,1536]{1,0:T(8,128)(2,1)} %get-tuple-element.67.near, bf16[512,1536]{1,0:T(8,128)(2,1)} %get-tuple-element.68.far, bf16[512,1536]{1,0:T(8,128)(2,1)} %get-tuple-element.69.ffn_far, ...), custom_call_target="tpu_custom_call" | custom-call | tf_op jit(solution)/shard_map/final/pallas_call | solution.py:1253
  422.7 0.0 copy-done.6
  422.7 0.0 copy-start.1
  422.7 0.7 copy.22
  423.4 0.7 copy.31
  424.1 0.7 copy.32
  424.8 0.7 copy.33
  425.5 0.9 copy.34
  426.4 0.9 copy.35
  427.3 0.9 copy.36
  (17 shorter events, 0.1 us)
Async XLA Ops:
  414.1 8.6 %copy-start.6 = (f32[192,128]{1,0:T(8,128)S(1)}, f32[192,128]{1,0:T(8,128)}, u32[]{:S(2)}) copy-start(f32[192,128]{1,0:T(8,128)} %get-tuple-element.80) | copy-start | bytes 294916
  414.1 9.3 %copy-start.4 = (f32[192,384]{1,0:T(8,128)S(1)}, f32[192,384]{1,0:T(8,128)}, u32[]{:S(2)}) copy-start(f32[192,384]{1,0:T(8,128)} %get-tuple-element.110) | copy-start | bytes 884740
  414.1 10.0 %copy-start.5 = (f32[192,256]{1,0:T(8,128)S(1)}, f32[192,256]{1,0:T(8,128)}, u32[]{:S(2)}) copy-start(f32[192,256]{1,0:T(8,128)} %get-tuple-element.111) | copy-start | bytes 589828
  414.1 10.7 %copy-start.3 = (f32[192,384]{1,0:T(8,128)S(1)}, f32[192,384]{1,0:T(8,128)}, u32[]{:S(2)}) copy-start(f32[192,384]{1,0:T(8,128)} %get-tuple-element.76) | copy-start | bytes 884740
  422.7 2.8 copy-start.2
  422.7 3.7 copy-start.1
  425.5 1.8 copy-start
where the time goes:
time: 434 us; the launch traced here: 429 us
  Pallas kernels  412 us (95%)
  local copies, waits for them, and re-layouts  9.1 us (2%)
  other arithmetic  6.46 us (1%)
    pallas_call x1, Pallas kernels, front(): pl.pallas_call(functools.partial(front_kernel, n_dp), in_specs=[vmem, hbm...  166 us
    pallas_call x1, Pallas kernels, back(): pl.pallas_call(functools.partial(back_kernel, n_dp), in_specs=[hbm] * 10...  124 us
    pallas_call x1, Pallas kernels, middle(): pl.pallas_call(functools.partial(middle_kernel, n_dp), in_specs=[hbm] * 7...  113 us

commit v1 on v0

--- a/solution.py
+++ b/solution.py
@@ -723,12 +723,12 @@
     for copy in load_far:
         copy.wait()
     lax.fori_loop(per, 2 * per, ffn, 0)
-    lax.fori_loop(0, per, back(per), 0)
+    lax.fori_loop(per // 2, per, back(per), 0)
     part_far = send(part.at[upper, :], far_recv, pair_sems, 0, near_id)
     part_far.start()
+    lax.fori_loop(0, per // 2, back(per), 0)
     for copy in load_near:
         copy.wait()
-    lax.fori_loop(0, 1, ffn, 0)
     part_far.wait_recv()
     fetch(far_recv, stage)
     sum_buf[...] = (part[:quarter, :].astype(F32) + stage[...].astype(F32)).astype(BF16)
@@ -753,7 +753,7 @@
 
     coming = load_go(0)
     coming_rows = load_rows(0)
-    lax.fori_loop(1, per, ffn, 0)
+    lax.fori_loop(0, per, ffn, 0)
     part_far.wait_send()
     lax.fori_loop(0, per, back(0), 0)
     part_near = send(part.at[upper, :], near_recv, pair_sems, 2, near_id)
@@ -779,6 +779,7 @@
     sum_far.wait_recv()
     fetch(x_recv, sum_buf)
     stores = []
+    ga_far = []
     for i in range(steps):
         for copy in coming_rows:
             copy.wait()
@@ -797,12 +798,23 @@
         ga_own[mine, :] = grad.astype(BF16)
         gain_two[0:1, :] += jnp.sum(grad_n * rows * scale, axis=0, keepdims=True)
         stores.append(local(rows_b.at[i % 2], grad_residual.at[rows_at(i), :]))
+        if i % (steps // 2) == steps // 2 - 1:
+            piece = len(ga_far)
+            at = piece * quarter // 2
+            ga_far.append(
+                send(
+                    ga_own.at[pl.ds(at, quarter // 2), :],
+                    ga_out.at[pl.ds(2 * quarter + at, quarter // 2), :],
+                    pair_sems,
+                    (3, 8)[piece],
+                    far_id,
+                )
+            )
+            ga_far[piece].start()
 
     def quarter_of(ref, j):
         return ref.at[pl.ds(j * quarter, quarter), :]
 
-    ga_far = send(ga_own, quarter_of(ga_out, 2), pair_sems, 3, far_id)
-    ga_far.start()
     ga_near = send(ga_own, quarter_of(ga_out, 1), pair_sems, 4, near_id)
     ga_near.start()
     stores_late = [local(ga_own, quarter_of(ga_out, 0))]
@@ -850,9 +862,20 @@
         stores.append(local(rows_a.at[i % 2], out_part.at[rows_at(i), :]))
     stores_late += stores[-2:]
 
-    ga_far.wait_recv()
-    ga_last = send(quarter_of(ga_out, 2), quarter_of(ga_out, 3), pair_sems, 7, near_id)
-    ga_last.start()
+    ga_last = []
+    for piece in (0, 1):
+        ga_far[piece].wait_recv()
+        at = piece * quarter // 2
+        ga_last.append(
+            send(
+                ga_out.at[pl.ds(2 * quarter + at, quarter // 2), :],
+                ga_out.at[pl.ds(3 * quarter + at, quarter // 2), :],
+                pair_sems,
+                (7, 9)[piece],
+                near_id,
+            )
+        )
+        ga_last[piece].start()
     save_d.wait()
     ring_d.add(3)
     ring_d.close(1)
@@ -863,10 +886,11 @@
     ring_d.end()
     ring_g.end()
     ga_near.wait_recv()
-    ga_last.wait_recv()
+    for copy in ga_last:
+        copy.wait_recv()
     for copy in stores_late:
         copy.wait()
-    for copy in (ga_far, ga_near, ga_last, part_near2):
+    for copy in (*ga_far, ga_near, *ga_last, part_near2):
         copy.wait_send()
 
 
@@ -914,7 +938,7 @@
             pltpu.VMEM((2, 128, width), F32),
             pltpu.VMEM((2, 128, width), F32),
             pltpu.SemaphoreType.DMA((2, 16)),
-            pltpu.SemaphoreType.DMA((2, 8)),
+            pltpu.SemaphoreType.DMA((2, 10)),
             pltpu.SemaphoreType.DMA((72,)),
         ],
         compiler_params=pltpu.CompilerParams(
@@ -1047,15 +1071,10 @@
         attend_back(t, i, q, do, mixed, lse, k, v, pos, valid, cos, sin, dqkv, dk_acc, dv_acc)
         return carry
 
-    lax.fori_loop(0, blocks * 4 // 8, attention, 0)
+    lax.fori_loop(0, blocks * 3 // 4, attention, 0)
+    ring_g.next(2)
     ring_o.next(1)
-    ring_g.next(2)
-    lax.fori_loop(blocks * 4 // 8, blocks * 6 // 8, attention, 0)
-    ring_o.next(2)
-    if ring:
-        result_d[...] = ring_d.result((0,))
-        store_d = local(result_d, down_out)
-    lax.fori_loop(blocks * 6 // 8, blocks, attention, 0)
+    lax.fori_loop(blocks * 3 // 4, blocks, attention, 0)
     a = dk_acc[...] * HEAD**-0.5
     dqkv[:, q_cols : q_cols + HEAD] = (a * cos[...] - pltpu.roll(a, HEAD // 2, 1) * sin[...]).astype(BF16)
     dqkv[:, q_cols + HEAD : kv_at] = dv_acc[...].astype(BF16)
@@ -1081,7 +1100,7 @@
     lax.fori_loop(0, per, grad_normed(per), 0)
     part_far = send(part.at[upper, :], far_recv, pair_sems, 1, near_id)
     part_far.start()
-    ring_o.next(3)
+    ring_o.next(2)
 
     def qkv_grad(i, carry):
         grads_a[block_rows(i), :] = dot_tn(acts[:, block_rows(i)], dqkv[...]).astype(BF16)
@@ -1089,6 +1108,7 @@
 
     lax.fori_loop(0, width // BLK, qkv_grad, 0)
     ring_a.start(1)
+    ring_g.next(3)
     part_far.wait_recv()
     fetch(far_recv, stage)
     sum_buf[...] = (part[:quarter, :].astype(F32) + stage[...].astype(F32)).astype(BF16)
@@ -1099,7 +1119,7 @@
     part_near = send(part.at[upper, :], near_recv, pair_sems, 3, near_id)
     part_near.start()
     stores = [local(part.at[pl.ds(0, quarter), :], part_own)]
-    ring_g.next(3)
+    ring_o.next(3)
 
     both = jnp.concatenate(
         [gain_acc[0:1, :] / gains[0:1, :], gain_two[0:1, :], jnp.zeros((HEAD - 2, width), F32)], axis=0
@@ -1109,15 +1129,18 @@
     ring_a.next(1)
     ring_s.next(1)
     if ring:
-        result_o[...] = ring_o.result()
-        stores.append(local(result_o, out_out))
+        result_d[...] = ring_d.result((0,))
+        stores.append(local(result_d, down_out))
     ring_a.next(2)
     ring_s.next(2)
     if ring:
+        result_o[...] = ring_o.result()
+        stores.append(local(result_o, out_out))
+    ring_a.next(3)
+    ring_s.next(3)
+    if ring:
         result_gu[...] = ring_g.result()
         stores += [local(result_gu.at[:, :units], gate_out), local(result_gu.at[:, units:], up_out)]
-    ring_a.next(3)
-    ring_s.next(3)
 
     if ring:
         shard = ring_a.result()
@@ -1145,8 +1168,6 @@
         stores.append(local(result_a.at[:, q_cols:], keyval_out))
         stores.append(local(grads_o, out_out))
         stores.append(local(gain_cols, gain_out))
-    if ring:
-        stores.append(store_d)
     for copy in stores:
         copy.wait()
     for each in (ring_g, ring_a, ring_o, ring_d):

time: 434 us -> 428 us (0.986)
  Pallas kernels: 412 us -> 406 us
where the time goes in v1:
time: 428 us; the launch traced here: 422 us
  Pallas kernels  406 us (95%)
  local copies, waits for them, and re-layouts  9.1 us (2%)
  other arithmetic  6.46 us (2%)
    pallas_call x1, Pallas kernels, front(): pl.pallas_call(functools.partial(front_kernel, n_dp), in_specs=[vmem, hbm...  166 us
    pallas_call x1, Pallas kernels, back(): pl.pallas_call(functools.partial(back_kernel, n_dp), in_specs=[hbm] * 10...  121 us
    pallas_call x1, Pallas kernels, middle(): pl.pallas_call(functools.partial(middle_kernel, n_dp), in_specs=[hbm] * 7...  110 us

profile of v1, /device:TPU:0, one launch (start us, length us, event | category | flops | bytes accessed | tf_op | source)
XLA Modules:
  0.0 422.3 jit_solution(13606484375317563323)
XLA Ops:
  0.7 0.6 maximum_bitcast_fusion.inverse
  1.3 0.7 broadcast_compare_fusion
  2.0 0.6 gather_fusion.1
  2.6 0.6 reshape.80.valid
  3.2 0.8 select_bitcast_fusion
  4.0 0.3 reduce-window.9
  4.3 0.1 slice.21
  4.4 0.1 slice_reduce_fusion
  4.5 0.1 reshape.77
  4.6 0.1 broadcast_bitcast_fusion
  4.7 0.6 gather_fusion
  5.3 0.6 reshape_reshape.3.pos
  5.9 0.8 copy.21
  6.7 1.8 fusion.1.shard_a
  8.6 2.1 pad_maximum_fusion.shard_g
  10.7 165.8 %front.1 = (f32[2048,128]{1,0:T(8,128)}, f32[2048,128]{1,0:T(8,128)}, bf16[1536,1152]{1,0:T(8,128)(2,1)}, bf16[1536,1152]{1,0:T(8,128)(2,1)}, bf16[1536,2304]{1,...) custom-call(bf16[512,1536]{1,0:T(8,128)(2,1)} %tokens.3, ...), custom_call_target="tpu_custom_call" | custom-call | flops 14495514624 | bytes 67108864 | tf_op jit(solution)/shard_map/front/pallas_call | solution.py:510
  176.5 110.3 %middle.1 = (bf16[1536,2304]{1,0:T(8,128)(2,1)}, bf16[1536,1152]{1,0:T(8,128)(2,1)}, f32[512,1536]{1,0:T(8,128)}, f32[8,1536]{1,0:T(8,128)}, bf16[2048,1536]{1,0...) custom-call(bf16[2048,1536]{1,0:T(8,128)(2,1)} %get-tuple-element.45, ...), custom_call_target="tpu_custom_call" | custom-call | flops 50734301184 | bytes 67108864 | tf_op jit(solution)/shard_map/middle/pallas_call | solution.py:906
  286.9 121.0 %back.1 = (bf16[512,1536]{1,0:T(8,128)(2,1)}, bf16[512,1536]{1,0:T(8,128)(2,1)}, bf16[512,1536]{1,0:T(8,128)(2,1)}, bf16[512,1536]{1,0:T(8,128)(2,1)}, f32[192,1...) custom-call(bf16[2048,1536]{1,0:T(8,128)(2,1)} %get-tuple-element.52, ...), custom_call_target="tpu_custom_call" | custom-call | flops 16911433728 | bytes 67108864 | tf_op jit(solution)/shard_map/back/pallas_call | solution.py:1194
  407.9 0.0 copy-start.6
  407.9 0.0 copy-start.4
  407.9 0.0 copy-start.5
  407.9 0.0 copy-start.3
  408.0 8.5 %final.1 = (bf16[512,1536]{1,0:T(8,128)(2,1)}, f32[512,1536]{1,0:T(8,128)}) custom-call(bf16[512,1536]{1,0:T(8,128)(2,1)} %get-tuple-element.66.own, bf16[512,1536]{1,0:T(8,128)(2,1)} %get-tuple-element.67.near, bf16[512,1536]{1,0:T(8,128)(2,1)} %get-tuple-element.68.far, bf16[512,1536]{1,0:T(8,128)(2,1)} %get-tuple-element.69.ffn_far, ...), custom_call_target="tpu_custom_call" | custom-call | tf_op jit(solution)/shard_map/final/pallas_call | solution.py:1274
  416.5 0.0 copy-done.6
  416.5 0.0 copy-start.1
  416.5 0.7 copy.22
  417.2 0.7 copy.31
  417.9 0.7 copy.32
  418.6 0.7 copy.33
  419.3 0.9 copy.34
  420.2 0.9 copy.35
  421.1 0.9 copy.36
  (17 shorter events, 0.1 us)
Async XLA Ops:
  407.9 8.6 %copy-start.6 = (f32[192,128]{1,0:T(8,128)S(1)}, f32[192,128]{1,0:T(8,128)}, u32[]{:S(2)}) copy-start(f32[192,128]{1,0:T(8,128)} %get-tuple-element.80) | copy-start | bytes 294916
  407.9 9.3 %copy-start.4 = (f32[192,384]{1,0:T(8,128)S(1)}, f32[192,384]{1,0:T(8,128)}, u32[]{:S(2)}) copy-start(f32[192,384]{1,0:T(8,128)} %get-tuple-element.110) | copy-start | bytes 884740
  407.9 10.0 %copy-start.5 = (f32[192,256]{1,0:T(8,128)S(1)}, f32[192,256]{1,0:T(8,128)}, u32[]{:S(2)}) copy-start(f32[192,256]{1,0:T(8,128)} %get-tuple-element.111) | copy-start | bytes 589828
  407.9 10.7 %copy-start.3 = (f32[192,384]{1,0:T(8,128)S(1)}, f32[192,384]{1,0:T(8,128)}, u32[]{:S(2)}) copy-start(f32[192,384]{1,0:T(8,128)} %get-tuple-element.76) | copy-start | bytes 884740
  416.5 2.8 copy-start.2
  416.5 3.7 copy-start.1
  419.3 1.8 copy-start

commit v2 on v1

--- a/solution.py
+++ b/solution.py
@@ -16,7 +16,7 @@
 F32 = jnp.float32
 BF16 = jnp.bfloat16
 MIB = 1 << 20
-EARLY = 2
+EARLY = 3
 
 NT = (((1,), (1,)), ((), ()))
 TN = (((0,), (0,)), ((), ()))

time: 428 us -> 428 us (level)
  no operation moved by 1% of the time
where the time goes in v2:
time: 428 us; the launch traced here: 422 us
  Pallas kernels  406 us (95%)
  local copies, waits for them, and re-layouts  9.1 us (2%)
  other arithmetic  6.46 us (2%)
    pallas_call x1, Pallas kernels, front(): pl.pallas_call(functools.partial(front_kernel, n_dp), in_specs=[vmem, hbm...  166 us
    pallas_call x1, Pallas kernels, back(): pl.pallas_call(functools.partial(back_kernel, n_dp), in_specs=[hbm] * 10...  119 us
    pallas_call x1, Pallas kernels, middle(): pl.pallas_call(functools.partial(middle_kernel, n_dp), in_specs=[hbm] * 7...  112 us

profile of v2, /device:TPU:0, one launch (start us, length us, event | category | flops | bytes accessed | tf_op | source)
XLA Modules:
  0.0 422.1 jit_solution(13959182471180270337)
XLA Ops:
  0.7 0.6 maximum_bitcast_fusion.inverse
  1.3 0.7 broadcast_compare_fusion
  2.0 0.6 gather_fusion.1
  2.6 0.6 reshape.80.valid
  3.2 0.8 select_bitcast_fusion
  4.0 0.3 reduce-window.9
  4.3 0.1 slice.21
  4.4 0.1 slice_reduce_fusion
  4.5 0.1 reshape.77
  4.6 0.1 broadcast_bitcast_fusion
  4.7 0.6 gather_fusion
  5.3 0.6 reshape_reshape.3.pos
  5.9 0.8 copy.21
  6.7 1.8 fusion.1.shard_a
  8.6 2.1 pad_maximum_fusion.shard_g
  10.7 165.8 %front.1 = (f32[2048,128]{1,0:T(8,128)}, f32[2048,128]{1,0:T(8,128)}, bf16[1536,1152]{1,0:T(8,128)(2,1)}, bf16[1536,1152]{1,0:T(8,128)(2,1)}, bf16[1536,2304]{1,...) custom-call(bf16[512,1536]{1,0:T(8,128)(2,1)} %tokens.3, ...), custom_call_target="tpu_custom_call" | custom-call | flops 14495514624 | bytes 67108864 | tf_op jit(solution)/shard_map/front/pallas_call | solution.py:510
  176.5 111.8 %middle.1 = (bf16[1536,2304]{1,0:T(8,128)(2,1)}, bf16[1536,1152]{1,0:T(8,128)(2,1)}, f32[512,1536]{1,0:T(8,128)}, f32[8,1536]{1,0:T(8,128)}, bf16[2048,1536]{1,0...) custom-call(bf16[2048,1536]{1,0:T(8,128)(2,1)} %get-tuple-element.45, ...), custom_call_target="tpu_custom_call" | custom-call | flops 50734301184 | bytes 67108864 | tf_op jit(solution)/shard_map/middle/pallas_call | solution.py:906
  288.4 119.3 %back.1 = (bf16[512,1536]{1,0:T(8,128)(2,1)}, bf16[512,1536]{1,0:T(8,128)(2,1)}, bf16[512,1536]{1,0:T(8,128)(2,1)}, bf16[512,1536]{1,0:T(8,128)(2,1)}, f32[192,1...) custom-call(bf16[2048,1536]{1,0:T(8,128)(2,1)} %get-tuple-element.52, ...), custom_call_target="tpu_custom_call" | custom-call | flops 16911433728 | bytes 67108864 | tf_op jit(solution)/shard_map/back/pallas_call | solution.py:1194
  407.7 0.0 copy-start.6
  407.7 0.0 copy-start.4
  407.7 0.0 copy-start.5
  407.7 0.0 copy-start.3
  407.8 8.5 %final.1 = (bf16[512,1536]{1,0:T(8,128)(2,1)}, f32[512,1536]{1,0:T(8,128)}) custom-call(bf16[512,1536]{1,0:T(8,128)(2,1)} %get-tuple-element.66.own, bf16[512,1536]{1,0:T(8,128)(2,1)} %get-tuple-element.67.near, bf16[512,1536]{1,0:T(8,128)(2,1)} %get-tuple-element.68.far, bf16[512,1536]{1,0:T(8,128)(2,1)} %get-tuple-element.69.ffn_far, ...), custom_call_target="tpu_custom_call" | custom-call | tf_op jit(solution)/shard_map/final/pallas_call | solution.py:1274
  416.3 0.0 copy-done.6
  416.3 0.7 copy.22
  417.0 0.7 copy.31
  417.7 0.7 copy.32
  418.4 0.7 copy.33
  419.1 0.9 copy.34
  420.0 0.0 copy-done.1
  420.0 0.9 copy.35
  420.9 0.9 copy.36
  (17 shorter events, 0.1 us)
Async XLA Ops:
  407.7 8.6 %copy-start.6 = (f32[192,128]{1,0:T(8,128)S(1)}, f32[192,128]{1,0:T(8,128)}, u32[]{:S(2)}) copy-start(f32[192,128]{1,0:T(8,128)} %get-tuple-element.80) | copy-start | bytes 294916
  407.7 9.3 %copy-start.4 = (f32[192,384]{1,0:T(8,128)S(1)}, f32[192,384]{1,0:T(8,128)}, u32[]{:S(2)}) copy-start(f32[192,384]{1,0:T(8,128)} %get-tuple-element.110) | copy-start | bytes 884740
  407.7 10.0 %copy-start.5 = (f32[192,256]{1,0:T(8,128)S(1)}, f32[192,256]{1,0:T(8,128)}, u32[]{:S(2)}) copy-start(f32[192,256]{1,0:T(8,128)} %get-tuple-element.111) | copy-start | bytes 589828
  407.7 10.7 %copy-start.3 = (f32[192,384]{1,0:T(8,128)S(1)}, f32[192,384]{1,0:T(8,128)}, u32[]{:S(2)}) copy-start(f32[192,384]{1,0:T(8,128)} %get-tuple-element.76) | copy-start | bytes 884740
  416.3 2.8 copy-start.2
  416.3 3.7 copy-start.1
  419.1 1.8 copy-start
